TPU v7x, 32 devices: a whole 2x2x4 slice. The times are simulated.
32 devices in a mesh: groups: 2 (over x), expert: 16 (over z, y, core).
Axes of the slice: x: 2, y: 2, z: 4, core: 2. Of those that a mesh axis runs over, the one named last changes fastest.
Arguments:
- tokens: bfloat16 [2, 2048, 2048], P(None, ('groups', 'expert')), parts along dimension 1, may hold values from -6 to 6
- route_ids: int32 [2, 2048, 2], P(None, ('groups', 'expert')), parts along dimension 1, may hold values from 0 to 15, as said below
- route_slots: int32 [2, 2048, 2], P(None, ('groups', 'expert')), parts along dimension 1, may hold values from 0 to 15, as said below
- mod_shift: float32 [4, 2048], P('groups'), parts along dimension 0, may hold values from -4 to 4
- mod_scale: float32 [4, 2048], P('groups'), parts along dimension 0, may hold values from -4 to 4
- mod_gate: float32 [4, 2048], P('groups'), parts along dimension 0, may hold values from 0.1 to 1.9
- guidance: float32 [2], P('groups'), parts along dimension 0, may hold values from 2 to 6
- router_weight: bfloat16 [2048, 16], replicated, may hold values from -0.125 to 0.125
- expert_gate: bfloat16 [16, 2048, 768], P('expert'), may hold values from -0.125 to 0.125
- expert_up: bfloat16 [16, 2048, 768], P('expert'), may hold values from -0.125 to 0.125
- expert_down: bfloat16 [16, 768, 2048], P('expert'), may hold values from -0.21875 to 0.21875
- shared_gate: bfloat16 [2048, 1408], P('expert'), may hold values from -0.125 to 0.125
- shared_up: bfloat16 [2048, 1408], P('expert'), may hold values from -0.125 to 0.125
- shared_down: bfloat16 [1408, 2048], P(None, 'expert'), may hold values from -0.15625 to 0.15625
- head_weight: bfloat16 [2048, 128], replicated, may hold values from -0.125 to 0.125
Outputs:
- hidden_out: bfloat16 [2, 2048, 2048], P(None, ('groups', 'expert')), parts along dimension 1
- guided: float32 [2048, 128], P(('groups', 'expert')), parts along dimension 0
There are 2 independent parts, one for each index of `groups`. A program takes and returns all parts, laid end to end along the dimension named above; an argument that names none is the same for every part. Nothing has to cross between parts.
Inputs may be any that keep to these rules, and one draw needn't show every extreme that they name: `route_ids`: for each half, the 64 tokens of one device name each expert at most 16 times in all; this is met by some expert on every device, and one expert is named 16 times by every device's tokens of both halves. A token's 2 experts differ. `route_slots`: within one half and one device, the choices that name one expert hold the distinct rows 0 to their number minus 1, in the same place as the expert in route_ids.
All inputs are finite; a program needn't handle non-finite values.
Results may differ from a plain program's by a relative error of at most 0.0067.
Values may be sent and summed in bfloat16 or wider, within the bound.
A program may use at most 128 MiB of HBM per device.

v0:
```python
import math

import jax
import jax.numpy as jnp
from jax import lax
from jax.sharding import PartitionSpec as P

epsilon = 1e-06


def layer_norm(values):
    center = values - jnp.mean(values, axis=-1, keepdims=True)
    spread = jnp.mean(center * center, axis=-1, keepdims=True)
    return center * lax.rsqrt(spread + epsilon)


def expert_block(received, w_gate, w_up, w_down):
    array_shape = received.shape
    local_count = w_gate.shape[0]
    middle = math.prod(array_shape[1:-1])
    row_block = received.reshape(
        array_shape[0] // local_count, local_count, middle, array_shape[-1]
    )
    gate_part = jnp.einsum("semd,edf->semf", row_block, w_gate, preferred_element_type=jnp.float32)
    up_part = jnp.einsum("semd,edf->semf", row_block, w_up, preferred_element_type=jnp.float32)
    hidden = (jax.nn.silu(gate_part) * up_part).astype(jnp.bfloat16)
    result = jnp.einsum("semf,efd->semd", hidden, w_down, preferred_element_type=jnp.float32)
    return result.astype(jnp.bfloat16).reshape(array_shape)


def dispatch_matrix(slot_place, slot_total):
    slot_index = jnp.arange(slot_total, dtype=jnp.int32)
    matches = slot_index[:, None, None] == slot_place[None, :, :]
    return jnp.sum(matches.astype(jnp.int32), axis=2).astype(jnp.bfloat16)


def local(
    tokens,
    route_ids,
    route_slots,
    mod_shift,
    mod_scale,
    mod_gate,
    guidance,
    router_weight,
    expert_gate,
    expert_up,
    expert_down,
    shared_gate,
    shared_up,
    shared_down,
    head_weight,
):
    model_width = tokens.shape[-1]
    per_half = tokens.shape[1]
    choices_each = route_ids.shape[2]
    experts = router_weight.shape[1]
    capacity = 2 * choices_each * per_half // experts
    inputs = tokens.astype(jnp.float32)
    modulated = (layer_norm(inputs) * (1.0 + mod_scale[:, None, :]) + mod_shift[:, None, :]).astype(
        jnp.bfloat16
    )
    flat_rows = modulated.reshape(2 * per_half, model_width)
    logits = jnp.dot(flat_rows, router_weight, preferred_element_type=jnp.float32).reshape(
        2, per_half, experts
    )
    picked = jnp.take_along_axis(logits, route_ids, axis=2)
    affinity = jax.nn.sigmoid(picked)
    weights = affinity / jnp.sum(affinity, axis=2, keepdims=True)
    full_gate, full_up, full_down = (
        lax.all_gather(shared_gate, "expert", axis=0, tiled=True),
        lax.all_gather(shared_up, "expert", axis=0, tiled=True),
        lax.all_gather(shared_down, "expert", axis=1, tiled=True),
    )
    gate_sum = jnp.dot(flat_rows, full_gate, preferred_element_type=jnp.float32)
    up_sum = jnp.dot(flat_rows, full_up, preferred_element_type=jnp.float32)
    shared_hidden = (jax.nn.silu(gate_sum) * up_sum).astype(jnp.bfloat16)
    shared = jnp.dot(shared_hidden, full_down, preferred_element_type=jnp.float32)
    shared = shared.reshape(2, per_half, model_width)
    half_index = jnp.arange(2, dtype=jnp.int32)
    slot_place = (route_ids * 2 + half_index[:, None, None]) * capacity + route_slots
    matrix = dispatch_matrix(slot_place.reshape(2 * per_half, choices_each), 2 * experts * capacity)
    outgoing = jnp.dot(matrix, flat_rows, preferred_element_type=jnp.float32).astype(jnp.bfloat16)
    outgoing = outgoing.reshape(experts, 2, capacity, model_width)
    answered = expert_block(
        lax.all_to_all(outgoing, "expert", split_axis=0, concat_axis=0, tiled=True),
        expert_gate,
        expert_up,
        expert_down,
    )
    returned = lax.all_to_all(answered, "expert", split_axis=0, concat_axis=0, tiled=True)
    chosen = jnp.take(returned.reshape(-1, model_width), slot_place.reshape(-1), axis=0)
    chosen = chosen.reshape(2, per_half, choices_each, model_width)
    routed = jnp.sum(weights[..., None] * chosen.astype(jnp.float32), axis=2)
    hidden_out = (inputs + mod_gate[:, None, :] * (routed + shared)).astype(jnp.bfloat16)
    final_norm = layer_norm(hidden_out.astype(jnp.float32)).astype(jnp.bfloat16)
    predicted = jnp.dot(
        final_norm.reshape(2 * per_half, model_width),
        head_weight,
        preferred_element_type=jnp.float32,
    )
    predicted = predicted.reshape(2, per_half, head_weight.shape[1])
    guided = predicted[1] + guidance[0] * (predicted[0] - predicted[1])
    return (hidden_out, guided)


def solution(mesh):
    in_specs = (
        P(None, ("groups", "expert"), None),
        P(None, ("groups", "expert"), None),
        P(None, ("groups", "expert"), None),
        P("groups", None),
        P("groups", None),
        P("groups", None),
        P("groups"),
        P(),
        P("expert", None, None),
        P("expert", None, None),
        P("expert", None, None),
        P("expert", None),
        P("expert", None),
        P(None, "expert"),
        P(),
    )
    out_specs = (P(None, ("groups", "expert"), None), P(("groups", "expert"), None))
    return jax.shard_map(local, mesh=mesh, in_specs=in_specs, out_specs=out_specs, check_vma=False)
```

profile of v0, /device:TPU:0, one launch (start us, length us, event | category | flops | bytes accessed | tf_op | source)
XLA Modules:
  0.0 277.4 jit_solution(16356291191841412131)
XLA Ops:
  7.3 0.7 all-gather.4.cloned.1.call-update
  8.0 0.7 all-gather.6.cloned.1.call-update
  8.8 0.7 all-gather.8.cloned.1.call-update
  9.4 1.2 convert_reduce_fusion
  10.6 1.3 fusion.23
  12.2 1.4 fusion.26
  13.7 0.7 convolution_convert_fusion
  14.4 89.1 %all_to_all.10 = bf16[16,2,16,2048]{3,2,1,0:T(8,128)(2,1)S(1)} all-to-all(bf16[16,2,16,2048]{3,2,1,0:T(8,128)(2,1)S(1)} %bitcast.95), channel_id=1, replica_groups=mesh['groups'=2,'expert'=16] {'expert'}, dimensions={0} | all-to-all | bytes 4194304 | tf_op jit(solution)/shard_map/all_to_all | solution.py:86
  103.5 1.3 copy-done.3
  104.9 3.0 %fusion.4 = f32[16,32,768]{2,1,0:T(8,128)} fusion(bf16[16,32,2048]{2,1,0:T(8,128)(2,1)S(1)} %bitcast.100, bf16[1,2048,768]{2,1,0:T(8,128)(2,1)S(1)} %copy-done.11), kind=kOutput, calls=%fused_computation.6 | convolution fusion | flops 1610612736 | bytes 6815744 | tf_op jit(solution)/shard_map/semd,edf->semf/dot_general | solution.py:24
  107.8 8.3 %fusion.6 = bf16[16,32,2048]{2,1,0:T(8,128)(2,1)} fusion(bf16[1,768,2048]{2,1,0:T(8,128)(2,1)S(1)} %copy-done, bf16[16,32,2048]{2,1,0:T(8,128)(2,1)} %bitcast.101, bf16[1,2048,768]{2,1,0:T(8,128)(2,1)} %param.24, f32[16,32,768]{2,1,0:T(8,128)} %fusion.4), kind=kOutput, calls=%fused_computation.9 | convolution fusion | flops 3224633344 | bytes 12058624 | tf_op jit(solution)/shard_map/semf,efd->semd/dot_general | solution.py:27
  116.1 4.8 %all-to-all-start.1 = ((bf16[16,2,16,2048]{3,2,1,0:T(8,128)(2,1)}), bf16[16,2,16,2048]{3,2,1,0:T(8,128)(2,1)}, u32[]{:S(2)}, u32[]{:S(2)}) async-start(bf16[16,2,16,2048]{3,2,1,0:T(8,128)(2,1)} %bitcast.99), calls=%async_computation.1 | async-start | bytes 4194304 | tf_op jit(solution)/shard_map/all_to_all | solution.py:91
  120.9 0.1 copy.45
  121.0 0.1 reshape.153
  121.3 0.1 reshape.164
  121.4 1.4 fusion.35
  122.8 2.5 gather_fusion.1
  125.3 0.1 reshape.167
  125.6 0.1 copy.42
  125.7 0.1 copy.43
  126.5 57.0 %all-to-all-done.1 = bf16[16,2,16,2048]{3,2,1,0:T(8,128)(2,1)} async-done(((bf16[16,2,16,2048]{3,2,1,0:T(8,128)(2,1)}), bf16[16,2,16,2048]{3,2,1,0:T(8,128)(2,1)}, u32[]{:S(2)}, u32[]{:S(2)}) %all-to-all-start.1) | async-done | bytes 2097184 | tf_op jit(solution)/shard_map/all_to_all | solution.py:91
  183.5 5.2 %gather_fusion = bf16[256,2048]{1,0:T(8,128)(2,1)} fusion(bf16[512,2048]{1,0:T(8,128)(2,1)} %bitcast.24, s32[1024]{0:T(1024)S(1)} %pad_clamp_fusion), kind=kCustom, calls=%fused_computation | custom fusion | bytes 2098176 | tf_op jit(solution)/shard_map/jit(_take)/gather | solution.py:92
  188.7 2.5 gather.12
  191.2 7.2 %multiply_reduce_fusion = f32[2,64,2048]{2,1,0:T(8,128)} fusion(bf16[2,64,2,2048]{3,2,1,0:T(2,128)(2,1)} %gather.12, pred[2,64,2]{2,1,0:T(8,128)(4,1)S(1)} %copy.43, f32[2,64,2]{2,1,0:T(8,128)S(1)} %copy.42), kind=kLoop, calls=%fused_computation.12 | loop fusion | flops 1835008 | bytes 2098432 | tf_op jit(solution)/shard_map/reduce_sum | solution.py:94
  198.5 4.7 %fusion.43 = f32[128,1408]{1,0:T(8,128)} fusion(bf16[128,2048]{1,0:T(8,128)(2,1)} %bitcast.97, bf16[2048,1408]{1,0:T(8,128)(2,1)} %all-gather.4.cloned.1.call-done), kind=kOutput, calls=%fused_computation.67 | convolution fusion | flops 738197504 | bytes 7012352 | tf_op jit(solution)/shard_map/dot_general | solution.py:75
  203.1 56.5 %all-gather.8.cloned.1.call-done = bf16[1408,2048]{1,0:T(8,128)(2,1)} async-done(((bf16[1408,128]{1,0:T(8,128)(2,1)}), bf16[1408,2048]{1,0:T(8,128)(2,1)}) %all-gather.8.cloned.1.call-update) | async-done | bytes 5767184 | tf_op jit(solution)/shard_map/all_gather | solution.py:73
  259.7 7.6 %fusion.32 = f32[128,2048]{1,0:T(8,128)} fusion(bf16[1408,2048]{1,0:T(8,128)(2,1)} %all-gather.8.cloned.1.call-done, bf16[128,2048]{1,0:T(8,128)(2,1)} %bitcast.98, bf16[2048,1408]{1,0:T(8,128)(2,1)} %all-gather.6.cloned.1.call-done, f32[128,1408]{1,0:T(8,128)} %fusion.43), kind=kOutput, calls=%fused_computation.38 | convolution fusion | flops 1477476352 | bytes 13828096 | tf_op jit(solution)/shard_map/dot_general | solution.py:78
  267.3 2.0 convert_reduce_fusion.1
  269.3 0.3 fusion.27
  269.6 0.3 fusion.28
  269.9 0.3 fusion.44
  270.2 0.6 fusion.38
  (44 shorter events, 0.6 us)
Async XLA Ops:
  7.2 100.7 %copy-start = (bf16[1,768,2048]{2,1,0:T(8,128)(2,1)S(1)}, bf16[1,768,2048]{2,1,0:T(8,128)(2,1)}, u32[]{:S(2)}) copy-start(bf16[1,768,2048]{2,1,0:T(8,128)(2,1)} %param.25) | copy-start | bytes 9437188
  7.2 4.8 %copy-start.9 = (f32[2,2048]{1,0:T(2,128)S(1)}, f32[2,2048]{1,0:T(2,128)}, u32[]{:S(2)}) copy-start(f32[2,2048]{1,0:T(2,128)} %param.19) | copy-start | bytes 49156
  7.2 4.8 %copy-start.6 = (s32[2,64,2]{1,2,0:T(2,128)S(1)}, s32[2,64,2]{1,2,0:T(2,128)}, u32[]{:S(2)}) copy-start(s32[2,64,2]{1,2,0:T(2,128)} %param.16) | copy-start | bytes 3076
  7.2 4.8 %copy-start.10 = (s32[2,64,2]{1,2,0:T(2,128)S(1)}, s32[2,64,2]{1,2,0:T(2,128)}, u32[]{:S(2)}) copy-start(s32[2,64,2]{1,2,0:T(2,128)} %param.17) | copy-start | bytes 3076
  7.2 5.0 %copy-start.7 = (f32[2,2048]{1,0:T(2,128)S(1)}, f32[2,2048]{1,0:T(2,128)}, u32[]{:S(2)}) copy-start(f32[2,2048]{1,0:T(2,128)} %param.18) | copy-start | bytes 49156
  7.2 191.2 %all-gather.4.cloned.1.call-start = ((), (), s32[]{:S(2)}) async-start(), calls=%async_computation.2 | async-start | bytes 6127616 | tf_op jit(solution)/shard_map/all_gather | solution.py:71
  8.0 195.2 %all-gather.6.cloned.1.call-start = ((), (), s32[]{:S(2)}) async-start(), calls=%async_computation.3 | async-start | bytes 6127616 | tf_op jit(solution)/shard_map/all_gather | solution.py:72
  8.7 251.0 %all-gather.8.cloned.1.call-start = ((), (), s32[]{:S(2)}) async-start(), calls=%async_computation.4 | async-start | bytes 6127616 | tf_op jit(solution)/shard_map/all_gather | solution.py:73
  13.6 89.9 %copy-start.1 = (bf16[2,64,2048]{2,1,0:T(8,128)(2,1)}, bf16[2,64,2048]{2,1,0:T(8,128)(2,1)S(1)}, u32[]{:S(2)}) copy-start(bf16[2,64,2048]{2,1,0:T(8,128)(2,1)S(1)} %fusion.26) | copy-start | bytes 1572868
  14.4 90.5 %copy-start.11 = (bf16[1,2048,768]{2,1,0:T(8,128)(2,1)S(1)}, bf16[1,2048,768]{2,1,0:T(8,128)(2,1)}, u32[]{:S(2)}) copy-start(bf16[1,2048,768]{2,1,0:T(8,128)(2,1)} %param.23) | copy-start | bytes 9437188
  103.5 1.3 copy-start.3
  116.1 5.3 %copy-start.5 = (bf16[2048,16]{0,1:T(8,128)(2,1)S(1)}, bf16[2048,16]{0,1:T(8,128)(2,1)}, u32[]{:S(2)}) copy-start(bf16[2048,16]{0,1:T(8,128)(2,1)} %param.22) | copy-start | bytes 196612
  116.1 67.4 %all-to-all-start.1 = ((bf16[16,2,16,2048]{3,2,1,0:T(8,128)(2,1)}), bf16[16,2,16,2048]{3,2,1,0:T(8,128)(2,1)}, u32[]{:S(2)}, u32[]{:S(2)}) async-start(bf16[16,2,16,2048]{3,2,1,0:T(8,128)(2,1)} %bitcast.99), calls=%async_computation.1 | async-start | bytes 4194304 | tf_op jit(solution)/shard_map/all_to_all | solution.py:91
  203.1 64.2 %copy-start.8 = (f32[2,2048]{1,0:T(2,128)S(1)}, f32[2,2048]{1,0:T(2,128)}, u32[]{:S(2)}) copy-start(f32[2,2048]{1,0:T(2,128)} %param.20) | copy-start | bytes 49156
  267.3 2.6 copy-start.4
  269.3 1.6 copy-start.2
Sparse Core Ops, SparseCore 0:
  10.3 93.4 all-gather.3
  106.1 88.0 all-gather.5
  196.3 63.3 all-gather.7
where the time goes:
time: 278 us; the launch traced here: 277 us
  waiting for transfers between devices  116 us (42%)
  blocking collectives  89.1 us (32%)
  matrix products  25.9 us (9%)
  between operations  14.7 us (5%)
  other arithmetic  14.6 us (5%)
  local copies, waits for them, and re-layouts  12.6 us (5%)
  starting transfers between devices  4.91 us (2%)
    all_to_all x1, blocking collectives, local(): lax.all_to_all(outgoing, 'expert', split_axis=0, concat_axis=0, tiled=True)  89.1 us
    all_to_all x1, waiting for transfers between devices, local(): lax.all_to_all(answered, 'expert', split_axis=0, concat_axis=0, tiled=True)  57 us
    all_gather x1, waiting for transfers between devices, local(): lax.all_gather(shared_down, 'expert', axis=1, tiled=True)  56.5 us
    dot_general x1, matrix products, expert_block(): jnp.einsum('semf,efd->semd', hidden, w_down, preferred_element_type=jnp.f...  8.28 us
    gather x2, local copies, waits for them, and re-layouts, local(): jnp.take(returned.reshape(-1, model_width), slot_place.reshape(-1), axis=0)  7.72 us
    dot_general x1, matrix products, local(): jnp.dot(shared_hidden, full_down, preferred_element_type=jnp.float32)  7.61 us
    reduce_sum x1, other arithmetic, local(): routed = jnp.sum(weights[..., None] * chosen.astype(jnp.float32), axis=2)  7.24 us
  transfers between devices with their start and end apart: 4, of which 2 were waited for; matrix products, arithmetic and copies ran while one was open for 15% of the time, Pallas kernels for 0%

commit v1 on v0

--- a/solution.py
+++ b/solution.py
@@ -1,11 +1,15 @@
+import functools
 import math
 
 import jax
 import jax.numpy as jnp
 from jax import lax
+from jax.experimental import pallas as pl
+from jax.experimental.pallas import tpu as pltpu
 from jax.sharding import PartitionSpec as P
 
 epsilon = 1e-06
+MESH = pl.DeviceIdType.MESH
 
 
 def layer_norm(values):
@@ -34,7 +38,393 @@
     return jnp.sum(matches.astype(jnp.int32), axis=2).astype(jnp.bfloat16)
 
 
+def tile_rows(count):
+    return -(-count // 16) * 16
+
+
+def stage_order(step, place, length):
+    if step == length - 1:
+        return place
+    down = length - 1 - step
+    down = down - jnp.where(down <= place, 1, 0)
+    up = step + jnp.where(place <= step, 1, 0)
+    return jnp.where(place < length // 2, down, up)
+
+
+def exchange_kernel(
+    n,
+    fp,
+    x_ref,
+    meta_ref,
+    wsend_ref,
+    eg_hbm,
+    eu_hbm,
+    ed_hbm,
+    out_ref,
+    xg,
+    mg,
+    w,
+    eg,
+    eu,
+    ed,
+    rows,
+    exs,
+    mid,
+    rw,
+    hid,
+    csend,
+    crecv,
+    keep,
+    ysend,
+    yrecv,
+    zsend,
+    zrecv,
+    load_sem,
+    x_send,
+    x_recv,
+    m_send,
+    m_recv,
+    w_send,
+    w_recv,
+    c_send,
+    c_recv,
+    y_send,
+    y_recv,
+    z_send,
+    z_recv,
+):
+    length = n // 4
+    me = lax.axis_index("expert")
+    z, y, c = me // 4, (me // 2) % 2, me % 2
+    tokens, width = x_ref.shape
+    per_block = rows.shape[0] // n
+    part = w.shape[1] // n
+    ff = eg.shape[1]
+    bf16 = jnp.bfloat16
+
+    def place(zz, yy, cc):
+        return zz * 4 + yy * 2 + cc
+
+    right, left = place(z + 1, y, c), place(z - 1, y, c)
+    across, sibling = place(z, 1 - y, c), place(z, y, 1 - c)
+
+    loads = [
+        pltpu.make_async_copy(src, dst, load_sem.at[i])
+        for i, (src, dst) in enumerate(((eg_hbm, eg), (eu_hbm, eu), (ed_hbm, ed)))
+    ]
+    for load in loads:
+        load.start()
+
+    barrier = pltpu.get_barrier_semaphore()
+    for step in range(1, n):
+        pl.semaphore_signal(
+            barrier, inc=1, device_id={"expert": lax.rem(me + step, n)}, device_id_type=MESH
+        )
+    xg[me] = x_ref[...]
+    mg[me] = meta_ref[...]
+    pl.semaphore_wait(barrier, n - 1)
+
+    def remote(src, dst, send, recv, target):
+        return pltpu.make_async_remote_copy(
+            src_ref=src,
+            dst_ref=dst,
+            send_sem=send,
+            recv_sem=recv,
+            device_id={"expert": target},
+            device_id_type=MESH,
+        )
+
+    def block_copies(which, way, target):
+        return (
+            remote(xg.at[which], xg.at[which], x_send.at[way, which], x_recv.at[which], target),
+            remote(mg.at[which], mg.at[which], m_send.at[way, which], m_recv.at[which], target),
+        )
+
+    def send_block(which, way, target):
+        for copy in block_copies(which, way, target):
+            copy.start()
+
+    def sent_block(which, way, target):
+        for copy in block_copies(which, way, target):
+            copy.wait_send()
+
+    def got_block(which):
+        for copy in block_copies(which, 0, sibling):
+            copy.wait_recv()
+
+    def weight_copy(step):
+        target = lax.rem(me + step, n)
+        return remote(
+            wsend_ref.at[target],
+            w.at[:, pl.ds(pl.multiple_of(me * part, part), part)],
+            w_send.at[step],
+            w_recv.at[me],
+            target,
+        )
+
+    def gate_block(which):
+        token_block = xg[which]
+        info = mg[which]
+        spot = lax.broadcasted_iota(jnp.int32, (per_block, tokens), 0).astype(jnp.float32)
+        base = (me * per_block).astype(jnp.float32)
+        first = spot == info[0:1, :] - base
+        second = spot == info[1:2, :] - base
+        pick = jnp.where(first | second, 1.0, 0.0).astype(bf16)
+        scale = jnp.where(first, info[2:3, :], 0.0) + jnp.where(second, info[3:4, :], 0.0)
+        spots = pl.ds(pl.multiple_of(which * per_block, per_block), per_block)
+        rows[spots, :] = jnp.dot(pick, token_block, preferred_element_type=jnp.float32).astype(bf16)
+        rw[spots, :] = jnp.broadcast_to(jnp.sum(scale, axis=1, keepdims=True), (per_block, 128))
+        both = lax.dot_general(
+            token_block, w[0 : 2 * fp, :], (((1,), (1,)), ((), ())), preferred_element_type=jnp.float32
+        )
+        gate, up = both[:, :fp], both[:, fp:]
+        hid[which] = (gate * jax.nn.sigmoid(gate) * up).astype(bf16)
+
+    def group(zz, index):
+        return place(zz, (y + index // 2) % 2, (c + index % 2) % 2)
+
+    for step in range(length + 1):
+        if step < length:
+            zs = stage_order(length - 1 - step, z, length)
+            which = place(zs, y, c)
+            if step > 0:
+                got_block(which)
+
+            @pl.when((zs <= z) & (z < length - 1))
+            def _():
+                send_block(which, 0, right)
+
+            @pl.when((zs >= z) & (z > 0))
+            def _():
+                send_block(which, 1, left)
+
+            send_block(which, 2, across)
+            send_block(which, 3, sibling)
+        if step == 0:
+            for other in range(1, n):
+                weight_copy(other).start()
+            w[:, pl.ds(pl.multiple_of(me * part, part), part)] = wsend_ref[me]
+        else:
+            zp = stage_order(length - step, z, length)
+            far = place(zp, 1 - y, c)
+            got_block(far)
+            send_block(far, 3, sibling)
+            got_block(place(zp, y, 1 - c))
+            got_block(place(zp, 1 - y, 1 - c))
+            if step == 1:
+                for other in range(1, n):
+                    source = lax.rem(me + other, n)
+                    remote(
+                        wsend_ref.at[0],
+                        w.at[:, pl.ds(pl.multiple_of(source * part, part), part)],
+                        w_send.at[other],
+                        w_recv.at[source],
+                        source,
+                    ).wait_recv()
+
+            def one_block(index, carry):
+                gate_block(group(zp, index))
+                return carry
+
+            lax.fori_loop(0, 4, one_block, 0)
+
+    for load in loads:
+        load.wait()
+    chunk = rows.shape[0] // 2
+    tile = ff // 3 if ff % 384 == 0 else ff
+
+    def expert_chunk(index, carry):
+        spots = pl.ds(pl.multiple_of(index * chunk, chunk), chunk)
+
+        def hidden_tile(at, inner):
+            columns = pl.ds(pl.multiple_of(at * tile, 128), tile)
+            taken = rows[spots, :]
+            gate = jnp.dot(taken, eg[:, columns], preferred_element_type=jnp.float32)
+            up = jnp.dot(taken, eu[:, columns], preferred_element_type=jnp.float32)
+            mid[:, columns] = (gate * jax.nn.sigmoid(gate) * up).astype(bf16)
+            return inner
+
+        lax.fori_loop(0, ff // tile, hidden_tile, 0)
+
+        def out_tile(at, inner):
+            columns = pl.ds(pl.multiple_of(at * 512, 512), 512)
+            result = jnp.dot(mid[...], ed[:, columns], preferred_element_type=jnp.float32)
+            exs[spots, columns] = (result * rw[spots, 0:1]).astype(bf16)
+            return inner
+
+        lax.fori_loop(0, width // 512, out_tile, 0)
+        return carry
+
+    lax.fori_loop(0, 2, expert_chunk, 0)
+
+    def partial_sum(which):
+        info = mg[which]
+        spot = lax.broadcasted_iota(jnp.int32, (per_block, tokens), 0).astype(jnp.float32)
+        base = (me * per_block).astype(jnp.float32)
+        pick = jnp.where(
+            (spot == info[0:1, :] - base) | (spot == info[1:2, :] - base), 1.0, 0.0
+        ).astype(bf16)
+        spots = pl.ds(pl.multiple_of(which * per_block, per_block), per_block)
+        routed = lax.dot_general(
+            pick, exs[spots, :], (((0,), (0,)), ((), ())), preferred_element_type=jnp.float32
+        )
+        return routed + jnp.dot(
+            hid[which], w[2 * fp : 3 * fp, :], preferred_element_type=jnp.float32
+        )
+
+    def core_copy(zz, yy):
+        at = yy * length + zz
+        return remote(csend.at[at], crecv.at[at], c_send.at[at], c_recv.at[at], sibling)
+
+    def y_copy(zz):
+        return remote(ysend.at[zz], yrecv.at[zz], y_send.at[zz], y_recv.at[zz], across)
+
+    def z_copy(way, zz, target):
+        return remote(zsend.at[zz], zrecv.at[way, zz], z_send.at[zz], z_recv.at[way, zz], target)
+
+    for step in range(length + 1):
+        if step < length:
+            zs = stage_order(step, z, length)
+            for yy in (1 - y, y):
+                csend[yy * length + zs] = partial_sum(place(zs, yy, 1 - c)).astype(bf16)
+                core_copy(zs, yy).start()
+            keep[zs] = partial_sum(place(zs, 1 - y, c))
+            core_copy(zs, 1 - y).wait_recv()
+            ysend[zs] = (keep[zs] + crecv[(1 - y) * length + zs].astype(jnp.float32)).astype(bf16)
+            y_copy(zs).start()
+            keep[zs] = partial_sum(place(zs, y, c))
+            core_copy(zs, y).wait_recv()
+            keep[zs] += crecv[y * length + zs].astype(jnp.float32)
+        if step > 0:
+            zp = stage_order(step - 1, z, length)
+            y_copy(zp).wait_recv()
+            keep[zp] += yrecv[zp].astype(jnp.float32)
+
+            @pl.when((zp >= z) & (z > 0))
+            def _():
+                z_copy(0, zp, left).wait_recv()
+                keep[zp] += zrecv[0, zp].astype(jnp.float32)
+
+            @pl.when((zp <= z) & (z < length - 1))
+            def _():
+                z_copy(1, zp, right).wait_recv()
+                keep[zp] += zrecv[1, zp].astype(jnp.float32)
+
+            if step < length:
+                zsend[zp] = keep[zp].astype(bf16)
+
+                @pl.when(zp > z)
+                def _():
+                    z_copy(0, zp, right).start()
+
+                @pl.when(zp < z)
+                def _():
+                    z_copy(1, zp, left).start()
+
+    out_ref[...] = keep[z]
+
+    for step in range(length):
+        zs = stage_order(step, z, length)
+        which = place(zs, y, c)
+
+        @pl.when((zs <= z) & (z < length - 1))
+        def _():
+            sent_block(which, 0, right)
+
+        @pl.when((zs >= z) & (z > 0))
+        def _():
+            sent_block(which, 1, left)
+
+        sent_block(which, 2, across)
+        sent_block(which, 3, sibling)
+        sent_block(place(zs, 1 - y, c), 3, sibling)
+        core_copy(zs, 1 - y).wait_send()
+        core_copy(zs, y).wait_send()
+        y_copy(zs).wait_send()
+        if step < length - 1:
+
+            @pl.when(zs > z)
+            def _():
+                z_copy(0, zs, right).wait_send()
+
+            @pl.when(zs < z)
+            def _():
+                z_copy(1, zs, left).wait_send()
+
+    for other in range(1, n):
+        weight_copy(other).wait_send()
+
+
+def exchange(n, fp, slots, flat_rows, meta, wsend, w_gate, w_up, w_down):
+    length = n // 4
+    tokens, width = flat_rows.shape
+    ff = w_gate.shape[1]
+    bf16, f32 = jnp.bfloat16, jnp.float32
+    whole = pl.BlockSpec(memory_space=pltpu.VMEM)
+    away = pl.BlockSpec(memory_space=pl.ANY)
+    sems = pltpu.SemaphoreType.DMA
+    return pl.pallas_call(
+        functools.partial(exchange_kernel, n, fp),
+        out_shape=jax.ShapeDtypeStruct((tokens, width), f32),
+        in_specs=[whole, whole, whole, away, away, away],
+        out_specs=whole,
+        scratch_shapes=[
+            pltpu.VMEM((n, tokens, width), bf16),
+            pltpu.VMEM((n,) + meta.shape, f32),
+            pltpu.VMEM((3 * fp, width), bf16),
+            pltpu.VMEM((width, ff), bf16),
+            pltpu.VMEM((width, ff), bf16),
+            pltpu.VMEM((ff, width), bf16),
+            pltpu.VMEM((n * slots, width), bf16),
+            pltpu.VMEM((n * slots, width), bf16),
+            pltpu.VMEM((n * slots // 2, ff), bf16),
+            pltpu.VMEM((n * slots, 128), f32),
+            pltpu.VMEM((n, tokens, fp), bf16),
+            pltpu.VMEM((2 * length, tokens, width), bf16),
+            pltpu.VMEM((2 * length, tokens, width), bf16),
+            pltpu.VMEM((length, tokens, width), f32),
+            pltpu.VMEM((length, tokens, width), bf16),
+            pltpu.VMEM((length, tokens, width), bf16),
+            pltpu.VMEM((length, tokens, width), bf16),
+            pltpu.VMEM((2, length, tokens, width), bf16),
+            sems((3,)),
+            sems((4, n)),
+            sems((n,)),
+            sems((4, n)),
+            sems((n,)),
+            sems((n,)),
+            sems((n,)),
+            sems((2 * length,)),
+            sems((2 * length,)),
+            sems((length,)),
+            sems((length,)),
+            sems((length,)),
+            sems((2, length)),
+        ],
+        compiler_params=pltpu.CompilerParams(
+            collective_id=0, has_side_effects=True, vmem_limit_bytes=60 * 1024 * 1024
+        ),
+    )(flat_rows, meta, wsend, w_gate, w_up, w_down)
+
+
+def fits(n, tokens, width, slots, ff, local_count, experts):
+    moved = n * tokens * width * 2 * 4
+    weights = 3 * width * ff * 2 + 2 * n * slots * width * 2
+    return (
+        n % 4 == 0
+        and experts == n
+        and local_count == 1
+        and tokens == 128
+        and width % (n * 128) == 0
+        and width % 512 == 0
+        and ff % 128 == 0
+        and slots % 16 == 0
+        and moved + weights < 56 * 1024 * 1024
+    )
+
+
 def local(
+    n,
     tokens,
     route_ids,
     route_slots,
@@ -67,32 +457,58 @@
     picked = jnp.take_along_axis(logits, route_ids, axis=2)
     affinity = jax.nn.sigmoid(picked)
     weights = affinity / jnp.sum(affinity, axis=2, keepdims=True)
-    full_gate, full_up, full_down = (
-        lax.all_gather(shared_gate, "expert", axis=0, tiled=True),
-        lax.all_gather(shared_up, "expert", axis=0, tiled=True),
-        lax.all_gather(shared_down, "expert", axis=1, tiled=True),
-    )
-    gate_sum = jnp.dot(flat_rows, full_gate, preferred_element_type=jnp.float32)
-    up_sum = jnp.dot(flat_rows, full_up, preferred_element_type=jnp.float32)
-    shared_hidden = (jax.nn.silu(gate_sum) * up_sum).astype(jnp.bfloat16)
-    shared = jnp.dot(shared_hidden, full_down, preferred_element_type=jnp.float32)
-    shared = shared.reshape(2, per_half, model_width)
     half_index = jnp.arange(2, dtype=jnp.int32)
     slot_place = (route_ids * 2 + half_index[:, None, None]) * capacity + route_slots
-    matrix = dispatch_matrix(slot_place.reshape(2 * per_half, choices_each), 2 * experts * capacity)
-    outgoing = jnp.dot(matrix, flat_rows, preferred_element_type=jnp.float32).astype(jnp.bfloat16)
-    outgoing = outgoing.reshape(experts, 2, capacity, model_width)
-    answered = expert_block(
-        lax.all_to_all(outgoing, "expert", split_axis=0, concat_axis=0, tiled=True),
-        expert_gate,
-        expert_up,
-        expert_down,
-    )
-    returned = lax.all_to_all(answered, "expert", split_axis=0, concat_axis=0, tiled=True)
-    chosen = jnp.take(returned.reshape(-1, model_width), slot_place.reshape(-1), axis=0)
-    chosen = chosen.reshape(2, per_half, choices_each, model_width)
-    routed = jnp.sum(weights[..., None] * chosen.astype(jnp.float32), axis=2)
-    hidden_out = (inputs + mod_gate[:, None, :] * (routed + shared)).astype(jnp.bfloat16)
+    slots = 2 * capacity
+    if choices_each == 2 and fits(
+        n,
+        2 * per_half,
+        model_width,
+        slots,
+        expert_gate.shape[2],
+        expert_gate.shape[0],
+        experts,
+    ):
+        share = shared_gate.shape[1] // n
+        fp = tile_rows(share)
+        pieces = [
+            jnp.pad(piece.reshape(n, share, -1), ((0, 0), (0, fp - share), (0, 0)))
+            for piece in (shared_gate.T, shared_up.T, shared_down)
+        ]
+        wsend = jnp.concatenate(pieces, axis=1)
+        flat_place = slot_place.reshape(2 * per_half, choices_each).astype(jnp.float32)
+        flat_weight = weights.reshape(2 * per_half, choices_each)
+        meta = jnp.concatenate([flat_place, flat_weight], axis=1).T
+        meta = jnp.pad(meta, ((0, 8 - meta.shape[0]), (0, 0)))
+        added = exchange(
+            n, fp, slots, flat_rows, meta, wsend, expert_gate[0], expert_up[0], expert_down[0]
+        ).reshape(2, per_half, model_width)
+    else:
+        full_gate, full_up, full_down = (
+            lax.all_gather(shared_gate, "expert", axis=0, tiled=True),
+            lax.all_gather(shared_up, "expert", axis=0, tiled=True),
+            lax.all_gather(shared_down, "expert", axis=1, tiled=True),
+        )
+        gate_sum = jnp.dot(flat_rows, full_gate, preferred_element_type=jnp.float32)
+        up_sum = jnp.dot(flat_rows, full_up, preferred_element_type=jnp.float32)
+        shared_hidden = (jax.nn.silu(gate_sum) * up_sum).astype(jnp.bfloat16)
+        shared = jnp.dot(shared_hidden, full_down, preferred_element_type=jnp.float32)
+        shared = shared.reshape(2, per_half, model_width)
+        matrix = dispatch_matrix(slot_place.reshape(2 * per_half, choices_each), 2 * experts * capacity)
+        outgoing = jnp.dot(matrix, flat_rows, preferred_element_type=jnp.float32).astype(jnp.bfloat16)
+        outgoing = outgoing.reshape(experts, 2, capacity, model_width)
+        answered = expert_block(
+            lax.all_to_all(outgoing, "expert", split_axis=0, concat_axis=0, tiled=True),
+            expert_gate,
+            expert_up,
+            expert_down,
+        )
+        returned = lax.all_to_all(answered, "expert", split_axis=0, concat_axis=0, tiled=True)
+        chosen = jnp.take(returned.reshape(-1, model_width), slot_place.reshape(-1), axis=0)
+        chosen = chosen.reshape(2, per_half, choices_each, model_width)
+        routed = jnp.sum(weights[..., None] * chosen.astype(jnp.float32), axis=2)
+        added = routed + shared
+    hidden_out = (inputs + mod_gate[:, None, :] * added).astype(jnp.bfloat16)
     final_norm = layer_norm(hidden_out.astype(jnp.float32)).astype(jnp.bfloat16)
     predicted = jnp.dot(
         final_norm.reshape(2 * per_half, model_width),
@@ -123,4 +539,5 @@
         P(),
     )
     out_specs = (P(None, ("groups", "expert"), None), P(("groups", "expert"), None))
-    return jax.shard_map(local, mesh=mesh, in_specs=in_specs, out_specs=out_specs, check_vma=False)
+    run = functools.partial(local, mesh.shape["expert"])
+    return jax.shard_map(run, mesh=mesh, in_specs=in_specs, out_specs=out_specs, check_vma=False)

time: 278 us -> 173 us (0.62)
  Pallas kernels: 0 us -> 157 us
  waiting for transfers between devices: 116 us -> 0 us
  blocking collectives: 89.1 us -> 0 us
  matrix products: 25.9 us -> 1.5 us
  between operations: 14.7 us -> 1.49 us
  local copies, waits for them, and re-layouts: 12.6 us -> 4.26 us
  other arithmetic: 14.6 us -> 8.66 us
  starting transfers between devices: 4.91 us -> 0 us
    pallas_call x0 -> x1, Pallas kernels: none -> 157 us  [exchange(): pl.pallas_call(functools.partial(exchange_kernel, n, fp), out_shape=jax.S...]
    all_to_all x1 -> x0, blocking collectives: 89.1 us -> none  [local(): lax.all_to_all(outgoing, 'expert', split_axis=0, concat_axis=0, tiled=True)]
    all_to_all x1 -> x0, waiting for transfers between devices: 57 us -> none  [local(): lax.all_to_all(answered, 'expert', split_axis=0, concat_axis=0, tiled=True)]
    all_gather x3 -> x0, waiting for transfers between devices: 56.5 us -> none  [the longest x1 56.5 us: local(): lax.all_gather(shared_down, 'expert', axis=1, tiled=True)]
    dot_general x5 -> x0, matrix products: 24.2 us -> none  [the longest x1 8.28 us: expert_block(): jnp.einsum('semf,efd->semd', hidden, w_down, preferred_element_type=jnp.f...]
    gather x2 -> x0, local copies, waits for them, and re-layouts: 7.72 us -> none  [local(): jnp.take(returned.reshape(-1, model_width), slot_place.reshape(-1), axis=0)]
    reduce_sum x2 -> x0, other arithmetic: 7.3 us -> none  [the longest x1 7.24 us: local(): routed = jnp.sum(weights[..., None] * chosen.astype(jnp.float32), axis=2)]
    all_to_all x1 -> x0, starting transfers between devices: 4.8 us -> none  [local(): lax.all_to_all(answered, 'expert', split_axis=0, concat_axis=0, tiled=True)]
  transfers between devices with their start and end apart: 4 -> 0, of which waited for: 2 -> 0; matrix products, arithmetic and copies ran while one was open for 15% -> 0% of each run, Pallas kernels for 0% -> 0%
where the time goes in v1:
time: 173 us
  Pallas kernels  157 us (91%)
  other arithmetic  8.66 us (5%)
  local copies, waits for them, and re-layouts  4.26 us (2%)
    pallas_call x1, Pallas kernels, exchange(): pl.pallas_call(functools.partial(exchange_kernel, n, fp), out_shape=jax.S...  157 us

profile of v1, /device:TPU:0, one launch (start us, length us, event | category | flops | bytes accessed | tf_op | source)
XLA Modules:
  0.0 173.1 jit_solution(4746455597325300855)
XLA Ops:
  0.6 0.0 copy-start
  0.7 1.3 convert_reduce_fusion
  1.9 1.3 fusion.10
  3.3 0.7 broadcast_add_fusion
  4.0 1.4 fusion.13
  5.4 0.0 copy-start.2
  5.4 1.2 fusion.17
  6.7 0.1 copy.34
  6.8 0.1 reshape.89
  6.9 0.0 copy-start.9
  7.0 0.0 copy-start.5
  7.0 0.0 copy-start.6
  7.0 0.0 copy-start.4
  7.0 2.4 %gather_fusion = f32[256]{0:T(256)S(1)} fusion(f32[2,64,16]{1,2,0:T(8,128)S(1)} %fusion.17, s32[256]{0:T(256)S(1)} %reshape.89), kind=kCustom, calls=%fused_computation | custom fusion | bytes 5120 | tf_op jit(solution)/shard_map/jit(take_along_axis)/gather | solution.py:457
  9.5 0.1 reshape.92
  9.6 0.1 copy.35
  9.7 0.1 add.79
  9.8 0.1 div.29
  9.9 0.0 copy-done.9
  9.9 0.1 convert_element_type.30
  10.0 0.6 pad.14.meta_ref
  10.6 0.0 copy-done.5
  10.6 0.2 copy.37
  10.8 0.0 copy-done.6
  10.9 0.2 copy.38
  11.1 1.1 fusion.9.wsend_ref
  12.2 157.1 %shard_map.158 = f32[128,2048]{1,0:T(8,128)} custom-call(bf16[128,2048]{1,0:T(8,128)(2,1)} %bitcast.31, f32[8,128]{1,0:T(8,128)} %pad.14.meta_ref, bf16[16,288,128]{2,1,0:T(8,128)(2,1)} %fusion.9.wsend_ref, bf16[2048,768]{1,0:T(8,128)(2,1)} %bitcast.33, bf16[2048,768]{1,0:T(8,128)(2,1)} %bitcast.34, bf16[768,2048]{1,0:T(8,128)(2,1)} %bitcast.35), custom_call_target="tpu_custom_call" | custom-call | tf_op jit(solution)/shard_map/pallas_call | solution.py:366
  169.4 1.5 convert_reduce_fusion.1
  170.8 0.3 fusion.14
  171.1 0.3 fusion.15
  171.5 0.3 fusion.23
  172.4 0.6 fusion.20
  (22 shorter events, 0.1 us)
Async XLA Ops:
  0.6 170.8 %copy-start = (bf16[2048,128]{1,0:T(8,128)(2,1)S(1)}, bf16[2048,128]{1,0:T(8,128)(2,1)}, u32[]{:S(2)}) copy-start(bf16[2048,128]{1,0:T(8,128)(2,1)} %param.29) | copy-start | bytes 1572868
  0.6 6.0 %copy-start.7 = (s32[2,64,2]{1,2,0:T(2,128)S(1)}, s32[2,64,2]{1,2,0:T(2,128)}, u32[]{:S(2)}) copy-start(s32[2,64,2]{1,2,0:T(2,128)} %param.16) | copy-start | bytes 3076
  5.4 4.0 %copy-start.2 = (bf16[2,64,2048]{2,1,0:T(8,128)(2,1)}, bf16[2,64,2048]{2,1,0:T(8,128)(2,1)S(1)}, u32[]{:S(2)}) copy-start(bf16[2,64,2048]{2,1,0:T(8,128)(2,1)S(1)} %fusion.13) | copy-start | bytes 1572868
  6.9 3.0 %copy-start.9 = (s32[2,64,2]{1,2,0:T(2,128)S(1)}, s32[2,64,2]{1,2,0:T(2,128)}, u32[]{:S(2)}) copy-start(s32[2,64,2]{1,2,0:T(2,128)} %param.17) | copy-start | bytes 3076
  7.0 3.7 %copy-start.5 = (bf16[128,1408]{1,0:T(8,128)(2,1)S(1)}, bf16[128,1408]{1,0:T(8,128)(2,1)}, u32[]{:S(2)}) copy-start(bf16[128,1408]{1,0:T(8,128)(2,1)} %param.26) | copy-start | bytes 1081348
  7.0 3.9 %copy-start.6 = (bf16[128,1408]{1,0:T(8,128)(2,1)S(1)}, bf16[128,1408]{1,0:T(8,128)(2,1)}, u32[]{:S(2)}) copy-start(bf16[128,1408]{1,0:T(8,128)(2,1)} %param.27) | copy-start | bytes 1081348
  7.0 4.1 %copy-start.4 = (bf16[1408,128]{1,0:T(8,128)(2,1)S(1)}, bf16[1408,128]{1,0:T(8,128)(2,1)}, u32[]{:S(2)}) copy-start(bf16[1408,128]{1,0:T(8,128)(2,1)} %param.28) | copy-start | bytes 1081348
  12.2 157.2 %copy-start.1 = (bf16[2,64,2048]{2,1,0:T(8,128)(2,1)S(1)}, bf16[2,64,2048]{2,1,0:T(8,128)(2,1)}, u32[]{:S(2)}) copy-start(bf16[2,64,2048]{2,1,0:T(8,128)(2,1)} %param.15) | copy-start | bytes 1572868
  12.2 157.2 %copy-start.8 = (f32[2,2048]{1,0:T(2,128)S(1)}, f32[2,2048]{1,0:T(2,128)}, u32[]{:S(2)}) copy-start(f32[2,2048]{1,0:T(2,128)} %param.20) | copy-start | bytes 49156
  170.8 2.2 %copy-start.3 = (bf16[2,64,2048]{2,1,0:T(8,128)(2,1)}, bf16[2,64,2048]{2,1,0:T(8,128)(2,1)S(1)}, u32[]{:S(2)}) copy-start(bf16[2,64,2048]{2,1,0:T(8,128)(2,1)S(1)} %get-tuple-element.3) | copy-start | bytes 1572868

commit v2 on v1

--- a/solution.py
+++ b/solution.py
@@ -53,6 +53,7 @@
 
 def exchange_kernel(
     n,
+    spread,
     fp,
     x_ref,
     meta_ref,
@@ -92,6 +93,8 @@
     y_recv,
     z_send,
     z_recv,
+    h_send,
+    h_recv,
 ):
     length = n // 4
     me = lax.axis_index("expert")
@@ -102,6 +105,9 @@
     ff = eg.shape[1]
     bf16 = jnp.bfloat16
 
+    def block(which):
+        return pl.ds(pl.multiple_of(which * tokens, tokens), tokens)
+
     def place(zz, yy, cc):
         return zz * 4 + yy * 2 + cc
 
@@ -120,9 +126,17 @@
         pl.semaphore_signal(
             barrier, inc=1, device_id={"expert": lax.rem(me + step, n)}, device_id_type=MESH
         )
-    xg[me] = x_ref[...]
+    group_at = lax.axis_index("groups")
+    for other in range(1, spread):
+        pl.semaphore_signal(
+            barrier,
+            inc=1,
+            device_id={"groups": lax.rem(group_at + other, spread)},
+            device_id_type=MESH,
+        )
+    xg[block(me), :] = x_ref[...]
     mg[me] = meta_ref[...]
-    pl.semaphore_wait(barrier, n - 1)
+    pl.semaphore_wait(barrier, n - 1 + spread - 1)
 
     def remote(src, dst, send, recv, target):
         return pltpu.make_async_remote_copy(
@@ -136,7 +150,7 @@
 
     def block_copies(which, way, target):
         return (
-            remote(xg.at[which], xg.at[which], x_send.at[way, which], x_recv.at[which], target),
+            remote(xg.at[block(which)], xg.at[block(which)], x_send.at[way, which], x_recv.at[which], target),
             remote(mg.at[which], mg.at[which], m_send.at[way, which], m_recv.at[which], target),
         )
 
@@ -152,18 +166,43 @@
         for copy in block_copies(which, 0, sibling):
             copy.wait_recv()
 
+    share = w.shape[0] // spread
+    own_share = pl.ds(pl.multiple_of(lax.rem(group_at, spread) * share, share), share)
+
+    def weight_columns(source):
+        return pl.ds(pl.multiple_of(source * part, part), part)
+
     def weight_copy(step):
         target = lax.rem(me + step, n)
         return remote(
-            wsend_ref.at[target],
-            w.at[:, pl.ds(pl.multiple_of(me * part, part), part)],
+            wsend_ref.at[target, own_share],
+            w.at[own_share, weight_columns(me)],
             w_send.at[step],
             w_recv.at[me],
             target,
         )
 
-    def gate_block(which):
-        token_block = xg[which]
+    def weight_landing(step):
+        source = lax.rem(me + step, n)
+        return remote(
+            wsend_ref.at[source, own_share],
+            w.at[own_share, weight_columns(source)],
+            w_send.at[step],
+            w_recv.at[source],
+            source,
+        )
+
+    def hand_on(step):
+        return pltpu.make_async_remote_copy(
+            src_ref=w.at[own_share],
+            dst_ref=w.at[own_share],
+            send_sem=h_send.at[step],
+            recv_sem=h_recv.at[step],
+            device_id={"groups": lax.rem(group_at + step, spread)},
+            device_id_type=MESH,
+        )
+
+    def route_rows(which):
         info = mg[which]
         spot = lax.broadcasted_iota(jnp.int32, (per_block, tokens), 0).astype(jnp.float32)
         base = (me * per_block).astype(jnp.float32)
@@ -172,69 +211,21 @@
         pick = jnp.where(first | second, 1.0, 0.0).astype(bf16)
         scale = jnp.where(first, info[2:3, :], 0.0) + jnp.where(second, info[3:4, :], 0.0)
         spots = pl.ds(pl.multiple_of(which * per_block, per_block), per_block)
-        rows[spots, :] = jnp.dot(pick, token_block, preferred_element_type=jnp.float32).astype(bf16)
+        rows[spots, :] = jnp.dot(
+            pick, xg[block(which), :], preferred_element_type=jnp.float32
+        ).astype(bf16)
         rw[spots, :] = jnp.broadcast_to(jnp.sum(scale, axis=1, keepdims=True), (per_block, 128))
-        both = lax.dot_general(
-            token_block, w[0 : 2 * fp, :], (((1,), (1,)), ((), ())), preferred_element_type=jnp.float32
-        )
-        gate, up = both[:, :fp], both[:, fp:]
-        hid[which] = (gate * jax.nn.sigmoid(gate) * up).astype(bf16)
-
-    def group(zz, index):
-        return place(zz, (y + index // 2) % 2, (c + index % 2) % 2)
-
-    for step in range(length + 1):
-        if step < length:
-            zs = stage_order(length - 1 - step, z, length)
-            which = place(zs, y, c)
-            if step > 0:
-                got_block(which)
-
-            @pl.when((zs <= z) & (z < length - 1))
-            def _():
-                send_block(which, 0, right)
-
-            @pl.when((zs >= z) & (z > 0))
-            def _():
-                send_block(which, 1, left)
-
-            send_block(which, 2, across)
-            send_block(which, 3, sibling)
-        if step == 0:
-            for other in range(1, n):
-                weight_copy(other).start()
-            w[:, pl.ds(pl.multiple_of(me * part, part), part)] = wsend_ref[me]
-        else:
-            zp = stage_order(length - step, z, length)
-            far = place(zp, 1 - y, c)
-            got_block(far)
-            send_block(far, 3, sibling)
-            got_block(place(zp, y, 1 - c))
-            got_block(place(zp, 1 - y, 1 - c))
-            if step == 1:
-                for other in range(1, n):
-                    source = lax.rem(me + other, n)
-                    remote(
-                        wsend_ref.at[0],
-                        w.at[:, pl.ds(pl.multiple_of(source * part, part), part)],
-                        w_send.at[other],
-                        w_recv.at[source],
-                        source,
-                    ).wait_recv()
-
-            def one_block(index, carry):
-                gate_block(group(zp, index))
-                return carry
-
-            lax.fori_loop(0, 4, one_block, 0)
-
-    for load in loads:
-        load.wait()
-    chunk = rows.shape[0] // 2
+
+    chunk = 4 * per_block
     tile = ff // 3 if ff % 384 == 0 else ff
 
-    def expert_chunk(index, carry):
-        spots = pl.ds(pl.multiple_of(index * chunk, chunk), chunk)
+    def expert_group(zz):
+        def one_block(index, carry):
+            route_rows(zz * 4 + index)
+            return carry
+
+        lax.fori_loop(0, 4, one_block, 0)
+        spots = pl.ds(pl.multiple_of(zz * chunk, chunk), chunk)
 
         def hidden_tile(at, inner):
             columns = pl.ds(pl.multiple_of(at * tile, 128), tile)
@@ -253,9 +244,14 @@
             return inner
 
         lax.fori_loop(0, width // 512, out_tile, 0)
-        return carry
-
-    lax.fori_loop(0, 2, expert_chunk, 0)
+
+    def shared_group(zz):
+        spots = pl.ds(pl.multiple_of(zz * 4 * tokens, tokens), 4 * tokens)
+        both = lax.dot_general(
+            xg[spots, :], w[0 : 2 * fp, :], (((1,), (1,)), ((), ())), preferred_element_type=jnp.float32
+        )
+        gate, up = both[:, :fp], both[:, fp:]
+        hid[spots, :] = (gate * jax.nn.sigmoid(gate) * up).astype(bf16)
 
     def partial_sum(which):
         info = mg[which]
@@ -269,7 +265,7 @@
             pick, exs[spots, :], (((0,), (0,)), ((), ())), preferred_element_type=jnp.float32
         )
         return routed + jnp.dot(
-            hid[which], w[2 * fp : 3 * fp, :], preferred_element_type=jnp.float32
+            hid[block(which), :], w[2 * fp : 3 * fp, :], preferred_element_type=jnp.float32
         )
 
     def core_copy(zz, yy):
@@ -282,44 +278,112 @@
     def z_copy(way, zz, target):
         return remote(zsend.at[zz], zrecv.at[way, zz], z_send.at[zz], z_recv.at[way, zz], target)
 
+    def y_step(step):
+        zs = stage_order(step, z, length)
+        for yy in (1 - y, y):
+            csend[yy * length + zs] = partial_sum(place(zs, yy, 1 - c)).astype(bf16)
+            core_copy(zs, yy).start()
+        keep[zs] = partial_sum(place(zs, 1 - y, c))
+        core_copy(zs, 1 - y).wait_recv()
+        ysend[zs] = (keep[zs] + crecv[(1 - y) * length + zs].astype(jnp.float32)).astype(bf16)
+        y_copy(zs).start()
+        keep[zs] = partial_sum(place(zs, y, c))
+        core_copy(zs, y).wait_recv()
+        keep[zs] += crecv[y * length + zs].astype(jnp.float32)
+
+    def z_step(step):
+        zp = stage_order(step, z, length)
+        y_copy(zp).wait_recv()
+        keep[zp] += yrecv[zp].astype(jnp.float32)
+
+        @pl.when((zp >= z) & (z > 0))
+        def _():
+            z_copy(0, zp, left).wait_recv()
+            keep[zp] += zrecv[0, zp].astype(jnp.float32)
+
+        @pl.when((zp <= z) & (z < length - 1))
+        def _():
+            z_copy(1, zp, right).wait_recv()
+            keep[zp] += zrecv[1, zp].astype(jnp.float32)
+
+        if step < length - 1:
+            zsend[zp] = keep[zp].astype(bf16)
+
+            @pl.when(zp > z)
+            def _():
+                z_copy(0, zp, right).start()
+
+            @pl.when(zp < z)
+            def _():
+                z_copy(1, zp, left).start()
+
+    def arrival(step):
+        return stage_order(length - 1 - step, z, length)
+
+    early = length - 2
     for step in range(length + 1):
         if step < length:
-            zs = stage_order(step, z, length)
-            for yy in (1 - y, y):
-                csend[yy * length + zs] = partial_sum(place(zs, yy, 1 - c)).astype(bf16)
-                core_copy(zs, yy).start()
-            keep[zs] = partial_sum(place(zs, 1 - y, c))
-            core_copy(zs, 1 - y).wait_recv()
-            ysend[zs] = (keep[zs] + crecv[(1 - y) * length + zs].astype(jnp.float32)).astype(bf16)
-            y_copy(zs).start()
-            keep[zs] = partial_sum(place(zs, y, c))
-            core_copy(zs, y).wait_recv()
-            keep[zs] += crecv[y * length + zs].astype(jnp.float32)
-        if step > 0:
-            zp = stage_order(step - 1, z, length)
-            y_copy(zp).wait_recv()
-            keep[zp] += yrecv[zp].astype(jnp.float32)
-
-            @pl.when((zp >= z) & (z > 0))
+            zs = arrival(step)
+            which = place(zs, y, c)
+            if step > 0:
+                got_block(which)
+
+            @pl.when((zs <= z) & (z < length - 1))
             def _():
-                z_copy(0, zp, left).wait_recv()
-                keep[zp] += zrecv[0, zp].astype(jnp.float32)
-
-            @pl.when((zp <= z) & (z < length - 1))
+                send_block(which, 0, right)
+
+            @pl.when((zs >= z) & (z > 0))
             def _():
-                z_copy(1, zp, right).wait_recv()
-                keep[zp] += zrecv[1, zp].astype(jnp.float32)
-
-            if step < length:
-                zsend[zp] = keep[zp].astype(bf16)
-
-                @pl.when(zp > z)
-                def _():
-                    z_copy(0, zp, right).start()
-
-                @pl.when(zp < z)
-                def _():
-                    z_copy(1, zp, left).start()
+                send_block(which, 1, left)
+
+            send_block(which, 2, across)
+            send_block(which, 3, sibling)
+        if step == 0:
+            for other in range(1, n):
+                weight_copy(other).start()
+            w[own_share, weight_columns(me)] = wsend_ref[me, own_share]
+            for load in loads:
+                load.wait()
+            continue
+        zp = arrival(step - 1)
+        far = place(zp, 1 - y, c)
+        got_block(far)
+        send_block(far, 3, sibling)
+        got_block(place(zp, y, 1 - c))
+        got_block(place(zp, 1 - y, 1 - c))
+        expert_group(zp)
+        if step == 1:
+            for other in range(1, n):
+                weight_landing(other).wait_recv()
+            for other in range(1, spread):
+                hand_on(other).start()
+        if step == length - 1:
+            for other in range(1, spread):
+                landed = lax.rem(group_at + spread - other, spread) * share
+                landed = pl.ds(pl.multiple_of(landed, share), share)
+                pltpu.make_async_remote_copy(
+                    src_ref=w.at[landed],
+                    dst_ref=w.at[landed],
+                    send_sem=h_send.at[other],
+                    recv_sem=h_recv.at[other],
+                    device_id={"groups": lax.rem(group_at + other, spread)},
+                    device_id_type=MESH,
+                ).wait_recv()
+            for done in range(length - 1):
+                shared_group(arrival(done))
+            y_step(early)
+        if step == length:
+            shared_group(zp)
+
+    later = [step for step in range(length) if step != early]
+    y_step(later[0])
+    sent = 0
+    for step in later[1:]:
+        y_step(step)
+        z_step(sent)
+        sent += 1
+    for step in range(sent, length):
+        z_step(step)
 
     out_ref[...] = keep[z]
 
@@ -353,9 +417,11 @@
 
     for other in range(1, n):
         weight_copy(other).wait_send()
-
-
-def exchange(n, fp, slots, flat_rows, meta, wsend, w_gate, w_up, w_down):
+    for other in range(1, spread):
+        hand_on(other).wait_send()
+
+
+def exchange(n, spread, fp, slots, flat_rows, meta, wsend, w_gate, w_up, w_down):
     length = n // 4
     tokens, width = flat_rows.shape
     ff = w_gate.shape[1]
@@ -364,12 +430,12 @@
     away = pl.BlockSpec(memory_space=pl.ANY)
     sems = pltpu.SemaphoreType.DMA
     return pl.pallas_call(
-        functools.partial(exchange_kernel, n, fp),
+        functools.partial(exchange_kernel, n, spread, fp),
         out_shape=jax.ShapeDtypeStruct((tokens, width), f32),
         in_specs=[whole, whole, whole, away, away, away],
         out_specs=whole,
         scratch_shapes=[
-            pltpu.VMEM((n, tokens, width), bf16),
+            pltpu.VMEM((n * tokens, width), bf16),
             pltpu.VMEM((n,) + meta.shape, f32),
             pltpu.VMEM((3 * fp, width), bf16),
             pltpu.VMEM((width, ff), bf16),
@@ -377,9 +443,9 @@
             pltpu.VMEM((ff, width), bf16),
             pltpu.VMEM((n * slots, width), bf16),
             pltpu.VMEM((n * slots, width), bf16),
-            pltpu.VMEM((n * slots // 2, ff), bf16),
+            pltpu.VMEM((4 * slots, ff), bf16),
             pltpu.VMEM((n * slots, 128), f32),
-            pltpu.VMEM((n, tokens, fp), bf16),
+            pltpu.VMEM((n * tokens, fp), bf16),
             pltpu.VMEM((2 * length, tokens, width), bf16),
             pltpu.VMEM((2 * length, tokens, width), bf16),
             pltpu.VMEM((length, tokens, width), f32),
@@ -400,6 +466,8 @@
             sems((length,)),
             sems((length,)),
             sems((2, length)),
+            sems((spread,)),
+            sems((spread,)),
         ],
         compiler_params=pltpu.CompilerParams(
             collective_id=0, has_side_effects=True, vmem_limit_bytes=60 * 1024 * 1024
@@ -412,6 +480,7 @@
     weights = 3 * width * ff * 2 + 2 * n * slots * width * 2
     return (
         n % 4 == 0
+        and n > 8
         and experts == n
         and local_count == 1
         and tokens == 128
@@ -425,6 +494,7 @@
 
 def local(
     n,
+    parts,
     tokens,
     route_ids,
     route_slots,
@@ -454,7 +524,8 @@
     logits = jnp.dot(flat_rows, router_weight, preferred_element_type=jnp.float32).reshape(
         2, per_half, experts
     )
-    picked = jnp.take_along_axis(logits, route_ids, axis=2)
+    chosen_expert = route_ids[..., None] == jnp.arange(experts, dtype=jnp.int32)
+    picked = jnp.sum(jnp.where(chosen_expert, logits[:, :, None, :], 0.0), axis=3)
     affinity = jax.nn.sigmoid(picked)
     weights = affinity / jnp.sum(affinity, axis=2, keepdims=True)
     half_index = jnp.arange(2, dtype=jnp.int32)
@@ -471,6 +542,7 @@
     ):
         share = shared_gate.shape[1] // n
         fp = tile_rows(share)
+        spread = parts if 3 * fp % (16 * parts) == 0 else 1
         pieces = [
             jnp.pad(piece.reshape(n, share, -1), ((0, 0), (0, fp - share), (0, 0)))
             for piece in (shared_gate.T, shared_up.T, shared_down)
@@ -481,7 +553,7 @@
         meta = jnp.concatenate([flat_place, flat_weight], axis=1).T
         meta = jnp.pad(meta, ((0, 8 - meta.shape[0]), (0, 0)))
         added = exchange(
-            n, fp, slots, flat_rows, meta, wsend, expert_gate[0], expert_up[0], expert_down[0]
+            n, spread, fp, slots, flat_rows, meta, wsend, expert_gate[0], expert_up[0], expert_down[0]
         ).reshape(2, per_half, model_width)
     else:
         full_gate, full_up, full_down = (
@@ -539,5 +611,5 @@
         P(),
     )
     out_specs = (P(None, ("groups", "expert"), None), P(("groups", "expert"), None))
-    run = functools.partial(local, mesh.shape["expert"])
+    run = functools.partial(local, mesh.shape["expert"], mesh.shape["groups"])
     return jax.shard_map(run, mesh=mesh, in_specs=in_specs, out_specs=out_specs, check_vma=False)

time: 173 us -> 147 us (0.85)
  Pallas kernels: 157 us -> 133 us
  local copies, waits for them, and re-layouts: 4.26 us -> 1.34 us
    pallas_call x1, Pallas kernels: 157 us -> 133 us  [exchange(): pl.pallas_call(functools.partial(exchange_kernel, n, spread, fp), out_sha...]
    gather x5 -> x0, local copies, waits for them, and re-layouts: 2.91 us -> none  [local(): picked = jnp.take_along_axis(logits, route_ids, axis=2)]
where the time goes in v2:
time: 147 us; the launch traced here: 146 us
  Pallas kernels  133 us (90%)
  other arithmetic  8.71 us (6%)
  matrix products  1.5 us (1%)
    pallas_call x1, Pallas kernels, exchange(): pl.pallas_call(functools.partial(exchange_kernel, n, spread, fp), out_sha...  133 us

profile of v2, /device:TPU:0, one launch (start us, length us, event | category | flops | bytes accessed | tf_op | source)
XLA Modules:
  0.0 146.2 jit_solution(6047294803726586459)
XLA Ops:
  0.6 0.0 copy-start
  0.6 0.0 copy-start.8
  0.7 0.0 copy-start.9
  0.7 0.0 copy-start.5
  0.7 0.0 copy-start.6
  0.7 0.0 copy-start.4
  0.7 1.3 convert_reduce_fusion
  2.0 1.3 fusion.10
  3.4 0.7 broadcast_add_fusion
  4.1 1.4 fusion.13
  5.5 0.0 copy-start.2
  5.5 1.2 fusion.17
  6.7 0.0 copy-done.8
  6.8 0.1 add.72
  6.9 0.1 div.29
  7.0 0.0 copy-done.9
  7.0 0.1 convert_element_type.30
  7.1 0.6 pad.14.meta_ref
  7.7 0.0 copy-done.5
  7.7 0.2 copy.24
  7.9 0.0 copy-done.6
  8.0 0.2 copy.25
  8.2 0.0 copy-done.4
  8.2 1.1 fusion.9.wsend_ref
  9.3 0.0 copy-done.2
  9.3 133.2 %shard_map.158 = f32[128,2048]{1,0:T(8,128)} custom-call(bf16[128,2048]{1,0:T(8,128)(2,1)} %bitcast.25, f32[8,128]{1,0:T(8,128)} %pad.14.meta_ref, bf16[16,288,128]{2,1,0:T(8,128)(2,1)} %fusion.9.wsend_ref, bf16[2048,768]{1,0:T(8,128)(2,1)} %bitcast.27, bf16[2048,768]{1,0:T(8,128)(2,1)} %bitcast.28, bf16[768,2048]{1,0:T(8,128)(2,1)} %bitcast.29), custom_call_target="tpu_custom_call" | custom-call | tf_op jit(solution)/shard_map/pallas_call | solution.py:432
  142.5 0.0 copy-done.1
  142.5 1.5 %convert_reduce_fusion.1 = (f32[2,64]{1,0:T(2,128)S(1)}, bf16[2,64,2048]{2,1,0:T(8,128)(2,1)S(1)}) fusion(f32[2,64,2048]{2,1,0:T(8,128)} %bitcast.26, f32[2,2048]{1,0:T(2,128)S(1)} %copy-done.7, bf16[2,64,2048]{2,1,0:T(8,128)(2,1)S(1)} %copy-done.1), kind=kLoop, calls=%fused_computation.12 | loop fusion | flops 1572736 | bytes 2114048 | tf_op jit(solution)/shard_map/reduce_sum | solution.py:16
  144.0 0.3 fusion.14
  144.3 0.3 fusion.15
  144.6 0.3 fusion.22
  145.6 0.6 fusion.20
  (17 shorter events, 0.1 us)
Async XLA Ops:
  0.6 144.0 %copy-start = (bf16[2048,128]{1,0:T(8,128)(2,1)S(1)}, bf16[2048,128]{1,0:T(8,128)(2,1)}, u32[]{:S(2)}) copy-start(bf16[2048,128]{1,0:T(8,128)(2,1)} %param.29) | copy-start | bytes 1572868
  0.6 6.1 %copy-start.8 = (s32[2,64,2]{1,2,0:T(2,128)S(1)}, s32[2,64,2]{1,2,0:T(2,128)}, u32[]{:S(2)}) copy-start(s32[2,64,2]{1,2,0:T(2,128)} %param.16) | copy-start | bytes 3076
  0.7 6.3 %copy-start.9 = (s32[2,64,2]{1,2,0:T(2,128)S(1)}, s32[2,64,2]{1,2,0:T(2,128)}, u32[]{:S(2)}) copy-start(s32[2,64,2]{1,2,0:T(2,128)} %param.17) | copy-start | bytes 3076
  0.7 7.1 %copy-start.5 = (bf16[128,1408]{1,0:T(8,128)(2,1)S(1)}, bf16[128,1408]{1,0:T(8,128)(2,1)}, u32[]{:S(2)}) copy-start(bf16[128,1408]{1,0:T(8,128)(2,1)} %param.26) | copy-start | bytes 1081348
  0.7 7.3 %copy-start.6 = (bf16[128,1408]{1,0:T(8,128)(2,1)S(1)}, bf16[128,1408]{1,0:T(8,128)(2,1)}, u32[]{:S(2)}) copy-start(bf16[128,1408]{1,0:T(8,128)(2,1)} %param.27) | copy-start | bytes 1081348
  0.7 7.5 %copy-start.4 = (bf16[1408,128]{1,0:T(8,128)(2,1)S(1)}, bf16[1408,128]{1,0:T(8,128)(2,1)}, u32[]{:S(2)}) copy-start(bf16[1408,128]{1,0:T(8,128)(2,1)} %param.28) | copy-start | bytes 1081348
  5.5 3.8 %copy-start.2 = (bf16[2,64,2048]{2,1,0:T(8,128)(2,1)}, bf16[2,64,2048]{2,1,0:T(8,128)(2,1)S(1)}, u32[]{:S(2)}) copy-start(bf16[2,64,2048]{2,1,0:T(8,128)(2,1)S(1)} %fusion.13) | copy-start | bytes 1572868
  9.3 133.2 %copy-start.1 = (bf16[2,64,2048]{2,1,0:T(8,128)(2,1)S(1)}, bf16[2,64,2048]{2,1,0:T(8,128)(2,1)}, u32[]{:S(2)}) copy-start(bf16[2,64,2048]{2,1,0:T(8,128)(2,1)} %param.15) | copy-start | bytes 1572868
  9.3 133.2 %copy-start.7 = (f32[2,2048]{1,0:T(2,128)S(1)}, f32[2,2048]{1,0:T(2,128)}, u32[]{:S(2)}) copy-start(f32[2,2048]{1,0:T(2,128)} %param.20) | copy-start | bytes 49156
  144.0 2.2 %copy-start.3 = (bf16[2,64,2048]{2,1,0:T(8,128)(2,1)}, bf16[2,64,2048]{2,1,0:T(8,128)(2,1)S(1)}, u32[]{:S(2)}) copy-start(bf16[2,64,2048]{2,1,0:T(8,128)(2,1)S(1)} %get-tuple-element.3) | copy-start | bytes 1572868

commit v3 on v2

--- a/solution.py
+++ b/solution.py
@@ -69,10 +69,10 @@
     eu,
     ed,
     rows,
-    exs,
+    rhs,
     mid,
     rw,
-    hid,
+    lhs,
     csend,
     crecv,
     keep,
@@ -202,12 +202,27 @@
             device_id_type=MESH,
         )
 
-    def route_rows(which):
+    chunk = 4 * per_block
+
+    def landed_share(step):
+        source = lax.rem(group_at + spread - step, spread)
+        landed = pl.ds(pl.multiple_of(source * share, share), share)
+        return pltpu.make_async_remote_copy(
+            src_ref=w.at[landed],
+            dst_ref=w.at[landed],
+            send_sem=h_send.at[step],
+            recv_sem=h_recv.at[step],
+            device_id={"groups": lax.rem(group_at + step, spread)},
+            device_id_type=MESH,
+        )
+
+    def route_rows(which, index):
         info = mg[which]
         spot = lax.broadcasted_iota(jnp.int32, (per_block, tokens), 0).astype(jnp.float32)
         base = (me * per_block).astype(jnp.float32)
-        first = spot == info[0:1, :] - base
-        second = spot == info[1:2, :] - base
+        near = info - base
+        first = spot == near[0:1, :]
+        second = spot == near[1:2, :]
         pick = jnp.where(first | second, 1.0, 0.0).astype(bf16)
         scale = jnp.where(first, info[2:3, :], 0.0) + jnp.where(second, info[3:4, :], 0.0)
         spots = pl.ds(pl.multiple_of(which * per_block, per_block), per_block)
@@ -215,13 +230,19 @@
             pick, xg[block(which), :], preferred_element_type=jnp.float32
         ).astype(bf16)
         rw[spots, :] = jnp.broadcast_to(jnp.sum(scale, axis=1, keepdims=True), (per_block, 128))
-
-    chunk = 4 * per_block
+        held = (near >= 0) & (near < per_block)
+        wide = jnp.where(held, near + (index * per_block).astype(jnp.float32), -1.0)
+        spread_spot = lax.broadcasted_iota(jnp.int32, (chunk, tokens), 0).astype(jnp.float32)
+        wide_pick = jnp.where(
+            (spread_spot == wide[0:1, :]) | (spread_spot == wide[1:2, :]), 1.0, 0.0
+        )
+        lhs[block(which), 0:chunk] = wide_pick.T.astype(bf16)
+
     tile = ff // 3 if ff % 384 == 0 else ff
 
     def expert_group(zz):
         def one_block(index, carry):
-            route_rows(zz * 4 + index)
+            route_rows(zz * 4 + index, index)
             return carry
 
         lax.fori_loop(0, 4, one_block, 0)
@@ -240,7 +261,7 @@
         def out_tile(at, inner):
             columns = pl.ds(pl.multiple_of(at * 512, 512), 512)
             result = jnp.dot(mid[...], ed[:, columns], preferred_element_type=jnp.float32)
-            exs[spots, columns] = (result * rw[spots, 0:1]).astype(bf16)
+            rhs[zz, 0:chunk, columns] = (result * rw[spots, 0:1]).astype(bf16)
             return inner
 
         lax.fori_loop(0, width // 512, out_tile, 0)
@@ -251,21 +272,14 @@
             xg[spots, :], w[0 : 2 * fp, :], (((1,), (1,)), ((), ())), preferred_element_type=jnp.float32
         )
         gate, up = both[:, :fp], both[:, fp:]
-        hid[spots, :] = (gate * jax.nn.sigmoid(gate) * up).astype(bf16)
-
-    def partial_sum(which):
-        info = mg[which]
-        spot = lax.broadcasted_iota(jnp.int32, (per_block, tokens), 0).astype(jnp.float32)
-        base = (me * per_block).astype(jnp.float32)
-        pick = jnp.where(
-            (spot == info[0:1, :] - base) | (spot == info[1:2, :] - base), 1.0, 0.0
-        ).astype(bf16)
-        spots = pl.ds(pl.multiple_of(which * per_block, per_block), per_block)
-        routed = lax.dot_general(
-            pick, exs[spots, :], (((0,), (0,)), ((), ())), preferred_element_type=jnp.float32
-        )
-        return routed + jnp.dot(
-            hid[block(which), :], w[2 * fp : 3 * fp, :], preferred_element_type=jnp.float32
+        lhs[spots, chunk : chunk + fp] = (gate * jax.nn.sigmoid(gate) * up).astype(bf16)
+        rhs[zz, chunk : chunk + fp, :] = w[2 * fp : 3 * fp, :]
+
+    def partial_sum(zz, yy, cc):
+        return jnp.dot(
+            lhs[block(place(zz, yy, cc)), 0 : chunk + fp],
+            rhs[zz],
+            preferred_element_type=jnp.float32,
         )
 
     def core_copy(zz, yy):
@@ -281,13 +295,13 @@
     def y_step(step):
         zs = stage_order(step, z, length)
         for yy in (1 - y, y):
-            csend[yy * length + zs] = partial_sum(place(zs, yy, 1 - c)).astype(bf16)
+            csend[yy * length + zs] = partial_sum(zs, yy, 1 - c).astype(bf16)
             core_copy(zs, yy).start()
-        keep[zs] = partial_sum(place(zs, 1 - y, c))
+        keep[zs] = partial_sum(zs, 1 - y, c)
         core_copy(zs, 1 - y).wait_recv()
         ysend[zs] = (keep[zs] + crecv[(1 - y) * length + zs].astype(jnp.float32)).astype(bf16)
         y_copy(zs).start()
-        keep[zs] = partial_sum(place(zs, y, c))
+        keep[zs] = partial_sum(zs, y, c)
         core_copy(zs, y).wait_recv()
         keep[zs] += crecv[y * length + zs].astype(jnp.float32)
 
@@ -345,6 +359,16 @@
             for load in loads:
                 load.wait()
             continue
+        if step == 2:
+            for other in range(1, n):
+                weight_landing(other).wait_recv()
+            for other in range(1, spread):
+                hand_on(other).start()
+        if step == length - 1:
+            for other in range(1, spread):
+                landed_share(other).wait_recv()
+            for done in range(length - 2):
+                shared_group(arrival(done))
         zp = arrival(step - 1)
         far = place(zp, 1 - y, c)
         got_block(far)
@@ -352,28 +376,10 @@
         got_block(place(zp, y, 1 - c))
         got_block(place(zp, 1 - y, 1 - c))
         expert_group(zp)
-        if step == 1:
-            for other in range(1, n):
-                weight_landing(other).wait_recv()
-            for other in range(1, spread):
-                hand_on(other).start()
+        if step >= length - 1:
+            shared_group(zp)
         if step == length - 1:
-            for other in range(1, spread):
-                landed = lax.rem(group_at + spread - other, spread) * share
-                landed = pl.ds(pl.multiple_of(landed, share), share)
-                pltpu.make_async_remote_copy(
-                    src_ref=w.at[landed],
-                    dst_ref=w.at[landed],
-                    send_sem=h_send.at[other],
-                    recv_sem=h_recv.at[other],
-                    device_id={"groups": lax.rem(group_at + other, spread)},
-                    device_id_type=MESH,
-                ).wait_recv()
-            for done in range(length - 1):
-                shared_group(arrival(done))
             y_step(early)
-        if step == length:
-            shared_group(zp)
 
     later = [step for step in range(length) if step != early]
     y_step(later[0])
@@ -442,10 +448,10 @@
             pltpu.VMEM((width, ff), bf16),
             pltpu.VMEM((ff, width), bf16),
             pltpu.VMEM((n * slots, width), bf16),
-            pltpu.VMEM((n * slots, width), bf16),
+            pltpu.VMEM((length, 4 * slots + fp, width), bf16),
             pltpu.VMEM((4 * slots, ff), bf16),
             pltpu.VMEM((n * slots, 128), f32),
-            pltpu.VMEM((n * tokens, fp), bf16),
+            pltpu.VMEM((n * tokens, -(-(4 * slots + fp) // 128) * 128), bf16),
             pltpu.VMEM((2 * length, tokens, width), bf16),
             pltpu.VMEM((2 * length, tokens, width), bf16),
             pltpu.VMEM((length, tokens, width), f32),
@@ -487,7 +493,7 @@
         and width % (n * 128) == 0
         and width % 512 == 0
         and ff % 128 == 0
-        and slots % 16 == 0
+        and slots % 32 == 0
         and moved + weights < 56 * 1024 * 1024
     )
 

time: 147 us -> 146 us (level)
  no operation moved by 1% of the time
where the time goes in v3:
time: 146 us
  Pallas kernels  133 us (91%)
  other arithmetic  8.71 us (6%)
  matrix products  1.5 us (1%)
    pallas_call x1, Pallas kernels, exchange(): pl.pallas_call(functools.partial(exchange_kernel, n, spread, fp), out_sha...  133 us

profile of v3, /device:TPU:0, one launch (start us, length us, event | category | flops | bytes accessed | tf_op | source)
XLA Modules:
  0.0 145.6 jit_solution(6896190972379027718)
XLA Ops:
  0.6 0.0 copy-start
  0.6 0.0 copy-start.8
  0.7 0.0 copy-start.9
  0.7 0.0 copy-start.5
  0.7 0.0 copy-start.6
  0.7 0.0 copy-start.4
  0.7 1.3 convert_reduce_fusion
  2.0 1.3 fusion.10
  3.4 0.7 broadcast_add_fusion
  4.1 1.4 fusion.13
  5.5 0.0 copy-start.2
  5.5 1.2 fusion.17
  6.7 0.0 copy-done.8
  6.8 0.1 add.72
  6.9 0.1 div.29
  7.0 0.0 copy-done.9
  7.0 0.1 convert_element_type.30
  7.1 0.6 pad.14.meta_ref
  7.7 0.0 copy-done.5
  7.7 0.2 copy.24
  7.9 0.0 copy-done.6
  8.0 0.2 copy.25
  8.2 0.0 copy-done.4
  8.2 1.1 fusion.9.wsend_ref
  9.3 0.0 copy-done.2
  9.3 132.6 %shard_map.158 = f32[128,2048]{1,0:T(8,128)} custom-call(bf16[128,2048]{1,0:T(8,128)(2,1)} %bitcast.25, f32[8,128]{1,0:T(8,128)} %pad.14.meta_ref, bf16[16,288,128]{2,1,0:T(8,128)(2,1)} %fusion.9.wsend_ref, bf16[2048,768]{1,0:T(8,128)(2,1)} %bitcast.27, bf16[2048,768]{1,0:T(8,128)(2,1)} %bitcast.28, bf16[768,2048]{1,0:T(8,128)(2,1)} %bitcast.29), custom_call_target="tpu_custom_call" | custom-call | tf_op jit(solution)/shard_map/pallas_call | solution.py:438
  141.9 0.0 copy-done.1
  141.9 1.5 %convert_reduce_fusion.1 = (f32[2,64]{1,0:T(2,128)S(1)}, bf16[2,64,2048]{2,1,0:T(8,128)(2,1)S(1)}) fusion(f32[2,64,2048]{2,1,0:T(8,128)} %bitcast.26, f32[2,2048]{1,0:T(2,128)S(1)} %copy-done.7, bf16[2,64,2048]{2,1,0:T(8,128)(2,1)S(1)} %copy-done.1), kind=kLoop, calls=%fused_computation.12 | loop fusion | flops 1572736 | bytes 2114048 | tf_op jit(solution)/shard_map/reduce_sum | solution.py:16
  143.4 0.3 fusion.14
  143.7 0.3 fusion.15
  144.0 0.3 fusion.22
  145.0 0.6 fusion.20
  (17 shorter events, 0.1 us)
Async XLA Ops:
  0.6 143.4 %copy-start = (bf16[2048,128]{1,0:T(8,128)(2,1)S(1)}, bf16[2048,128]{1,0:T(8,128)(2,1)}, u32[]{:S(2)}) copy-start(bf16[2048,128]{1,0:T(8,128)(2,1)} %param.29) | copy-start | bytes 1572868
  0.6 6.1 %copy-start.8 = (s32[2,64,2]{1,2,0:T(2,128)S(1)}, s32[2,64,2]{1,2,0:T(2,128)}, u32[]{:S(2)}) copy-start(s32[2,64,2]{1,2,0:T(2,128)} %param.16) | copy-start | bytes 3076
  0.7 6.3 %copy-start.9 = (s32[2,64,2]{1,2,0:T(2,128)S(1)}, s32[2,64,2]{1,2,0:T(2,128)}, u32[]{:S(2)}) copy-start(s32[2,64,2]{1,2,0:T(2,128)} %param.17) | copy-start | bytes 3076
  0.7 7.1 %copy-start.5 = (bf16[128,1408]{1,0:T(8,128)(2,1)S(1)}, bf16[128,1408]{1,0:T(8,128)(2,1)}, u32[]{:S(2)}) copy-start(bf16[128,1408]{1,0:T(8,128)(2,1)} %param.26) | copy-start | bytes 1081348
  0.7 7.3 %copy-start.6 = (bf16[128,1408]{1,0:T(8,128)(2,1)S(1)}, bf16[128,1408]{1,0:T(8,128)(2,1)}, u32[]{:S(2)}) copy-start(bf16[128,1408]{1,0:T(8,128)(2,1)} %param.27) | copy-start | bytes 1081348
  0.7 7.5 %copy-start.4 = (bf16[1408,128]{1,0:T(8,128)(2,1)S(1)}, bf16[1408,128]{1,0:T(8,128)(2,1)}, u32[]{:S(2)}) copy-start(bf16[1408,128]{1,0:T(8,128)(2,1)} %param.28) | copy-start | bytes 1081348
  5.5 3.8 %copy-start.2 = (bf16[2,64,2048]{2,1,0:T(8,128)(2,1)}, bf16[2,64,2048]{2,1,0:T(8,128)(2,1)S(1)}, u32[]{:S(2)}) copy-start(bf16[2,64,2048]{2,1,0:T(8,128)(2,1)S(1)} %fusion.13) | copy-start | bytes 1572868
  9.3 132.6 %copy-start.1 = (bf16[2,64,2048]{2,1,0:T(8,128)(2,1)S(1)}, bf16[2,64,2048]{2,1,0:T(8,128)(2,1)}, u32[]{:S(2)}) copy-start(bf16[2,64,2048]{2,1,0:T(8,128)(2,1)} %param.15) | copy-start | bytes 1572868
  9.3 132.6 %copy-start.7 = (f32[2,2048]{1,0:T(2,128)S(1)}, f32[2,2048]{1,0:T(2,128)}, u32[]{:S(2)}) copy-start(f32[2,2048]{1,0:T(2,128)} %param.20) | copy-start | bytes 49156
  143.4 2.2 %copy-start.3 = (bf16[2,64,2048]{2,1,0:T(8,128)(2,1)}, bf16[2,64,2048]{2,1,0:T(8,128)(2,1)S(1)}, u32[]{:S(2)}) copy-start(bf16[2,64,2048]{2,1,0:T(8,128)(2,1)S(1)} %get-tuple-element.3) | copy-start | bytes 1572868

commit v4 on v3

--- a/solution.py
+++ b/solution.py
@@ -57,6 +57,9 @@
     fp,
     x_ref,
     meta_ref,
+    shift_ref,
+    scale_ref,
+    router_ref,
     wsend_ref,
     eg_hbm,
     eu_hbm,
@@ -134,8 +137,32 @@
             device_id={"groups": lax.rem(group_at + other, spread)},
             device_id_type=MESH,
         )
-    xg[block(me), :] = x_ref[...]
-    mg[me] = meta_ref[...]
+    per_half = tokens // 2
+    for half in range(2):
+        values = x_ref[half * per_half : (half + 1) * per_half, :].astype(jnp.float32)
+        normed = layer_norm(values)
+        modulated = normed * (1.0 + scale_ref[half : half + 1, :]) + shift_ref[half : half + 1, :]
+        spot = pl.multiple_of(me * tokens + half * per_half, per_half)
+        xg[pl.ds(spot, per_half), :] = modulated.astype(bf16)
+    logits = lax.dot_general(
+        router_ref[...],
+        xg[block(me), :],
+        (((1,), (1,)), ((), ())),
+        preferred_element_type=jnp.float32,
+    )
+    chosen = meta_ref[...]
+    expert_row = lax.broadcasted_iota(jnp.int32, logits.shape, 0).astype(jnp.float32)
+    affinity = [
+        jax.nn.sigmoid(
+            jnp.sum(jnp.where(expert_row == chosen[k : k + 1, :], logits, 0.0), axis=0, keepdims=True)
+        )
+        for k in (2, 3)
+    ]
+    total = affinity[0] + affinity[1]
+    row_at = lax.broadcasted_iota(jnp.int32, chosen.shape, 0)
+    mg[me] = jnp.where(
+        row_at == 2, affinity[0] / total, jnp.where(row_at == 3, affinity[1] / total, chosen)
+    )
     pl.semaphore_wait(barrier, n - 1 + spread - 1)
 
     def remote(src, dst, send, recv, target):
@@ -427,7 +454,7 @@
         hand_on(other).wait_send()
 
 
-def exchange(n, spread, fp, slots, flat_rows, meta, wsend, w_gate, w_up, w_down):
+def exchange(n, spread, fp, slots, flat_rows, meta, shift, scale, router, wsend, w_gate, w_up, w_down):
     length = n // 4
     tokens, width = flat_rows.shape
     ff = w_gate.shape[1]
@@ -438,7 +465,7 @@
     return pl.pallas_call(
         functools.partial(exchange_kernel, n, spread, fp),
         out_shape=jax.ShapeDtypeStruct((tokens, width), f32),
-        in_specs=[whole, whole, whole, away, away, away],
+        in_specs=[whole] * 6 + [away] * 3,
         out_specs=whole,
         scratch_shapes=[
             pltpu.VMEM((n * tokens, width), bf16),
@@ -478,7 +505,7 @@
         compiler_params=pltpu.CompilerParams(
             collective_id=0, has_side_effects=True, vmem_limit_bytes=60 * 1024 * 1024
         ),
-    )(flat_rows, meta, wsend, w_gate, w_up, w_down)
+    )(flat_rows, meta, shift, scale, router, wsend, w_gate, w_up, w_down)
 
 
 def fits(n, tokens, width, slots, ff, local_count, experts):
@@ -523,17 +550,6 @@
     experts = router_weight.shape[1]
     capacity = 2 * choices_each * per_half // experts
     inputs = tokens.astype(jnp.float32)
-    modulated = (layer_norm(inputs) * (1.0 + mod_scale[:, None, :]) + mod_shift[:, None, :]).astype(
-        jnp.bfloat16
-    )
-    flat_rows = modulated.reshape(2 * per_half, model_width)
-    logits = jnp.dot(flat_rows, router_weight, preferred_element_type=jnp.float32).reshape(
-        2, per_half, experts
-    )
-    chosen_expert = route_ids[..., None] == jnp.arange(experts, dtype=jnp.int32)
-    picked = jnp.sum(jnp.where(chosen_expert, logits[:, :, None, :], 0.0), axis=3)
-    affinity = jax.nn.sigmoid(picked)
-    weights = affinity / jnp.sum(affinity, axis=2, keepdims=True)
     half_index = jnp.arange(2, dtype=jnp.int32)
     slot_place = (route_ids * 2 + half_index[:, None, None]) * capacity + route_slots
     slots = 2 * capacity
@@ -555,13 +571,36 @@
         ]
         wsend = jnp.concatenate(pieces, axis=1)
         flat_place = slot_place.reshape(2 * per_half, choices_each).astype(jnp.float32)
-        flat_weight = weights.reshape(2 * per_half, choices_each)
-        meta = jnp.concatenate([flat_place, flat_weight], axis=1).T
+        flat_ids = route_ids.reshape(2 * per_half, choices_each).astype(jnp.float32)
+        meta = jnp.concatenate([flat_place, flat_ids], axis=1).T
         meta = jnp.pad(meta, ((0, 8 - meta.shape[0]), (0, 0)))
         added = exchange(
-            n, spread, fp, slots, flat_rows, meta, wsend, expert_gate[0], expert_up[0], expert_down[0]
+            n,
+            spread,
+            fp,
+            slots,
+            tokens.reshape(2 * per_half, model_width),
+            meta,
+            mod_shift,
+            mod_scale,
+            router_weight.T,
+            wsend,
+            expert_gate[0],
+            expert_up[0],
+            expert_down[0],
         ).reshape(2, per_half, model_width)
     else:
+        modulated = (layer_norm(inputs) * (1.0 + mod_scale[:, None, :]) + mod_shift[:, None, :]).astype(
+            jnp.bfloat16
+        )
+        flat_rows = modulated.reshape(2 * per_half, model_width)
+        logits = jnp.dot(flat_rows, router_weight, preferred_element_type=jnp.float32).reshape(
+            2, per_half, experts
+        )
+        chosen_expert = route_ids[..., None] == jnp.arange(experts, dtype=jnp.int32)
+        picked = jnp.sum(jnp.where(chosen_expert, logits[:, :, None, :], 0.0), axis=3)
+        affinity = jax.nn.sigmoid(picked)
+        weights = affinity / jnp.sum(affinity, axis=2, keepdims=True)
         full_gate, full_up, full_down = (
             lax.all_gather(shared_gate, "expert", axis=0, tiled=True),
             lax.all_gather(shared_up, "expert", axis=0, tiled=True),

time: 146 us -> 143 us (0.979)
  other arithmetic: 8.71 us -> 5.6 us
  local copies, waits for them, and re-layouts: 1.34 us -> 3.19 us
    transpose x2, local copies, waits for them, and re-layouts: 0.44 us -> 2.4 us  [local(): pieces = [jnp.pad(piece.reshape(n, share, -1), ((0, 0), (0, fp - share),...]
where the time goes in v4:
time: 143 us
  Pallas kernels  133 us (93%)
  other arithmetic  5.6 us (4%)
  local copies, waits for them, and re-layouts  3.19 us (2%)
    pallas_call x1, Pallas kernels, exchange(): pl.pallas_call(functools.partial(exchange_kernel, n, spread, fp), out_sha...  133 us

profile of v4, /device:TPU:0, one launch (start us, length us, event | category | flops | bytes accessed | tf_op | source)
XLA Modules:
  0.0 143.1 jit_solution(2009131627122376761)
XLA Ops:
  0.6 0.0 copy-start
  0.6 0.8 add_convert_fusion.1
  1.4 0.1 convert_element_type.32
  1.5 0.1 convert_element_type.34
  1.6 0.6 pad.14.meta_ref
  2.2 1.2 copy.19
  3.4 1.2 copy.20
  4.6 2.1 %fusion.7.wsend_ref = bf16[16,288,128]{2,1,0:T(8,128)(2,1)} fusion(bf16[16,88,128]{2,1,0:T(8,128)(2,1)} %bitcast.30, bf16[16,88,128]{2,1,0:T(8,128)(2,1)S(1)} %bitcast.29, bf16[16,88,128]{2,1,0:T(8,128)(2,1)S(1)} %bitcast.28), kind=kLoop, calls=%fused_computation.13 | loop fusion | flops 8257536 | bytes 2260992 | tf_op jit(solution)/shard_map/concatenate | solution.py:572
  6.7 0.0 copy-start.2
  6.7 0.0 copy-start.3
  6.7 132.6 %shard_map.158 = f32[128,2048]{1,0:T(8,128)} custom-call(bf16[128,2048]{1,0:T(8,128)(2,1)} %bitcast.26, f32[8,128]{1,0:T(8,128)} %pad.14.meta_ref, f32[2,2048]{1,0:T(2,128)} %shift_ref.1, f32[2,2048]{1,0:T(2,128)} %scale_ref.1, bf16[16,2048]{1,0:T(8,128)(2,1)} %bitcast.33, bf16[16,288,128]{2,1,0:T(8,128)(2,1)} %fusion.7.wsend_ref, ...), custom_call_target="tpu_custom_call" | custom-call | tf_op jit(solution)/shard_map/pallas_call | solution.py:465
  139.4 0.0 copy-done.2
  139.4 0.0 copy-done.3
  139.4 1.5 %convert_reduce_fusion = (f32[2,64]{1,0:T(2,128)S(1)}, bf16[2,64,2048]{2,1,0:T(8,128)(2,1)S(1)}) fusion(f32[2,64,2048]{2,1,0:T(8,128)} %bitcast.22, f32[2,2048]{1,0:T(2,128)S(1)} %copy-done.3, bf16[2,64,2048]{2,1,0:T(8,128)(2,1)S(1)} %copy-done.2), kind=kLoop, calls=%fused_computation.9 | loop fusion | flops 1572736 | bytes 2114048 | tf_op jit(solution)/shard_map/reduce_sum | solution.py:16
  140.9 0.0 copy-start.1
  140.9 0.3 fusion.8
  141.2 0.3 fusion.9
  141.5 0.0 copy-done
  141.5 0.3 fusion.12
  142.4 0.6 fusion.11
  143.1 0.0 copy-done.1
  (5 shorter events, 0.0 us)
Async XLA Ops:
  0.6 140.9 %copy-start = (bf16[2048,128]{1,0:T(8,128)(2,1)S(1)}, bf16[2048,128]{1,0:T(8,128)(2,1)}, u32[]{:S(2)}) copy-start(bf16[2048,128]{1,0:T(8,128)(2,1)} %param.29) | copy-start | bytes 1572868
  6.7 132.6 %copy-start.2 = (bf16[2,64,2048]{2,1,0:T(8,128)(2,1)S(1)}, bf16[2,64,2048]{2,1,0:T(8,128)(2,1)}, u32[]{:S(2)}) copy-start(bf16[2,64,2048]{2,1,0:T(8,128)(2,1)} %param.15) | copy-start | bytes 1572868
  6.7 132.7 %copy-start.3 = (f32[2,2048]{1,0:T(2,128)S(1)}, f32[2,2048]{1,0:T(2,128)}, u32[]{:S(2)}) copy-start(f32[2,2048]{1,0:T(2,128)} %param.20) | copy-start | bytes 49156
  140.9 2.2 %copy-start.1 = (bf16[2,64,2048]{2,1,0:T(8,128)(2,1)}, bf16[2,64,2048]{2,1,0:T(8,128)(2,1)S(1)}, u32[]{:S(2)}) copy-start(bf16[2,64,2048]{2,1,0:T(8,128)(2,1)S(1)} %get-tuple-element.3) | copy-start | bytes 1572868
